TPU v7x, 256 devices: a whole 4x4x8 slice. The times are simulated.
256 devices in a mesh: frames: 128 (over z, y, x_hi, core), mp: 2 (over x_lo).
Axes of the slice: x: 4 (x_hi: 2, x_lo: 2; x = x_hi * 2 + x_lo), y: 4, z: 8, core: 2. Of those that a mesh axis runs over, the one named last changes fastest.
Arguments:
- normed: bfloat16 [128, 512, 1536], P('frames'), may hold values from -24 to 24
- out_grad: bfloat16 [128, 512, 768], P('frames', None, 'mp'), may hold values from -24 to 24
- w_qkv: bfloat16 [1536, 3, 768], P('frames', None, 'mp'), may hold values from -0.15625 to 0.15625
Outputs:
- input_grad: bfloat16 [128, 512, 1536], P('frames', None, 'mp')
- weight_grad: float32 [1536, 3, 768], P('frames', None, 'mp')
All inputs are finite; a program needn't handle non-finite values.
Results may differ from a plain program's by a relative error of at most 0.012.
Values may be sent and summed in bfloat16 or wider, within the bound.
No kernel may reach another device: no remote copies, remote signals or barrier semaphores. Data moves between devices by JAX's collectives and lax.ppermute only.
A program may use at most 128 MiB of HBM per device.

v0:
```python
import jax
import jax.numpy as jnp
from jax import lax
from jax.sharding import PartitionSpec as P

HEAD_DIM = 64


def attend(proj, upstream):
    steps_len, count, _, half = proj.shape
    heads = half // HEAD_DIM
    scale = HEAD_DIM ** (-0.5)
    shaped = proj.reshape(steps_len, count, 3, heads, HEAD_DIM)
    query = shaped[:, :, 0]
    keys = shaped[:, :, 1]
    values = shaped[:, :, 2]
    upper = upstream.reshape(steps_len, count, heads, HEAD_DIM)
    scores = jnp.einsum("fpne,gpne->pnfg", query, keys, preferred_element_type=jnp.float32) * scale
    weights = jnp.exp(scores)
    weights = weights / jnp.sum(weights, axis=-1, keepdims=True)
    probs = weights.astype(jnp.bfloat16)
    dvalues = jnp.einsum(
        "pnfg,fpne->gpne", probs, upper, preferred_element_type=jnp.float32
    ).astype(jnp.bfloat16)
    dprobs = jnp.einsum("fpne,gpne->pnfg", upper, values, preferred_element_type=jnp.float32)
    center = jnp.sum(weights * dprobs, axis=-1, keepdims=True)
    dscores = (weights * (dprobs - center) * scale).astype(jnp.bfloat16)
    dquery = jnp.einsum(
        "pnfg,gpne->fpne", dscores, keys, preferred_element_type=jnp.float32
    ).astype(jnp.bfloat16)
    dkeys = jnp.einsum(
        "pnfg,fpne->gpne", dscores, query, preferred_element_type=jnp.float32
    ).astype(jnp.bfloat16)
    return jnp.stack([dquery, dkeys, dvalues], axis=2).reshape(steps_len, count, 3, half)


def on_device(normed, out_grad, w_qkv):
    frames_dev, patches, width = normed.shape
    half = out_grad.shape[2]
    out_cols = width // lax.axis_size("mp")
    groups = lax.axis_size("frames")
    per_group = patches // groups
    steps_len = frames_dev * groups
    gathered = lax.all_gather(w_qkv, "frames", axis=0, tiled=True).reshape(width, 3 * half)
    upstream = out_grad.reshape(frames_dev, groups, per_group, half)
    token_rows = normed.reshape(frames_dev * patches, width)
    proj = jnp.dot(token_rows, gathered, preferred_element_type=jnp.float32).astype(jnp.bfloat16)
    proj = proj.reshape(frames_dev, groups, per_group, 3 * half)
    proj_piece = lax.all_to_all(proj, "frames", split_axis=1, concat_axis=0, tiled=True)
    upper_piece = lax.all_to_all(upstream, "frames", split_axis=1, concat_axis=0, tiled=True)
    count = proj_piece.shape[2]
    result = attend(
        proj_piece.reshape(steps_len, count, 3, half), upper_piece.reshape(steps_len, count, half)
    )
    patched = result.reshape(steps_len, 1, count, 3 * half)
    grads = lax.all_to_all(patched, "frames", split_axis=0, concat_axis=1, tiled=True).reshape(
        frames_dev * patches, 3 * half
    )
    rows_owned = w_qkv.shape[0]
    term = lax.dot_general(
        token_rows, grads, (((0,), (0,)), ((), ())), preferred_element_type=jnp.float32
    )
    summed_weight = lax.psum_scatter(
        term.reshape(lax.axis_size("frames") * rows_owned, 3, half),
        "frames",
        scatter_dimension=0,
        tiled=True,
    )
    partial_value = lax.dot_general(
        grads, gathered, (((1,), (1,)), ((), ())), preferred_element_type=jnp.float32
    )
    weight_grad = summed_weight * (1.0 / steps_len)
    summed = lax.psum_scatter(partial_value, "mp", scatter_dimension=1, tiled=True).astype(
        jnp.bfloat16
    )
    input_grad = summed.reshape(frames_dev, patches, out_cols)
    return (input_grad, weight_grad)


def solution(mesh):
    in_specs = (P("frames", None, None), P("frames", None, "mp"), P("frames", None, "mp"))
    out_specs = (P("frames", None, "mp"), P("frames", None, "mp"))
    return jax.shard_map(
        on_device, mesh=mesh, in_specs=in_specs, out_specs=out_specs, check_vma=False
    )
```

profile of v0, /device:TPU:6, one launch (start us, length us, event | category | flops | bytes accessed | tf_op | source)
XLA Modules:
  0.0 1607.6 jit_solution(17580815624956892219)
XLA Ops:
  7.2 0.0 copy-start
  7.2 0.0 all-gather.2.cloned.1.call-start
  7.2 0.7 all-gather.2.cloned.1.call-update
  7.9 1.8 reshape.42
  9.8 15.4 all-to-all-start.1
  25.2 109.4 %all-gather.2.cloned.1.call-done = bf16[1536,3,384]{2,1,0:T(4,128)(2,1)} async-done(((bf16[12,3,384]{2,1,0:T(4,128)(2,1)}), bf16[1536,3,384]{2,1,0:T(4,128)(2,1)}) %all-gather.2.cloned.1.call-update) | async-done | bytes 3538960 | tf_op jit(solution)/shard_map/all_gather | solution.py:44
  134.5 8.0 copy.33
  142.5 0.0 copy-done
  142.5 4.2 convolution_convert_fusion
  146.7 1.2 reshape.41
  147.9 0.0 all-to-all-done.1
  147.9 11.0 all-to-all-start
  158.9 0.0 reduce-scatter.2.cloned.1.call-start
  159.0 0.3 copy.39
  159.3 31.6 %all-to-all-done = bf16[1,128,4,1152]{3,2,0,1:T(4,128)(2,1)S(1)} async-done(((bf16[1,128,4,1152]{3,2,0,1:T(4,128)(2,1)}), bf16[1,128,4,1152]{3,2,0,1:T(4,128)(2,1)S(1)}, u32[]{:S(2)}, u32[]{:S(2)}) %all-to-all-start) | async-done | bytes 1179680 | tf_op jit(solution)/shard_map/all_to_all | solution.py:49
  190.9 2.1 copy.35
  192.9 0.0 copy-start.1
  192.9 2.9 fusion.12
  195.9 0.0 copy-done.1
  195.9 1.6 fusion.14
  197.5 3.4 fusion.7
  200.8 4.2 fusion.8
  205.1 0.0 copy-start.3
  205.1 2.1 fusion.9
  207.2 0.0 copy-done.3
  207.2 0.1 pad_maximum_fusion
  207.3 0.1 copy.43
  207.4 2.1 copy.44
  209.5 41.1 %all_to_all.12 = bf16[128,1,4,1152]{3,2,1,0:T(4,128)(2,1)S(1)} all-to-all(bf16[128,1,4,1152]{3,2,1,0:T(4,128)(2,1)} %copy.44), channel_id=1, replica_groups=mesh['frames'=128,'mp'=2] {'frames'}, dimensions={0} | all-to-all | bytes 2359296 | tf_op jit(solution)/shard_map/all_to_all | solution.py:56
  250.5 1.2 reshape.43
  251.7 6.2 fusion.19
  257.9 0.0 copy-start.2
  257.9 0.0 reduce-scatter.2.cloned.1.call-update
  258.0 0.0 all-reduce.3.cloned.1.call-start
  258.0 1.2 copy-done.2
  259.2 4.9 fusion.4
  264.1 11.0 copy.45
  275.0 0.0 copy-start.4
  275.0 0.0 all-reduce.3.cloned.1.call-update
  275.1 0.6 copy-done.4
  275.7 0.6 dynamic-slice
  276.9 24.8 %reduce-scatter.2.cloned.1.call-done = f32[512,768]{1,0:T(8,128)} async-done(((f32[512,1536]{1,0:T(8,128)}), f32[512,768]{1,0:T(8,128)}) %reduce-scatter.2.cloned.1.call-update) | async-done | bytes 1572880 | tf_op jit(solution)/shard_map/reduce_scatter | solution.py:73
  301.7 2.4 convert_bitcast_fusion
  304.1 1295.5 %all-reduce.3.cloned.1.call-done = f32[1536,3,384]{2,1,0:T(4,128)} async-done(((f32[1536,3,384]{2,1,0:T(4,128)}), f32[1536,3,384]{2,1,0:T(4,128)}) %all-reduce.3.cloned.1.call-update) | async-done | bytes 7077904
  1599.6 1.5 dynamic-slice_multiply_fusion
Async XLA Ops:
  7.2 135.3 %copy-start = (bf16[1,512,1536]{2,1,0:T(8,128)(2,1)S(1)}, bf16[1,512,1536]{2,1,0:T(8,128)(2,1)}, u32[]{:S(2)}) copy-start(bf16[1,512,1536]{2,1,0:T(8,128)(2,1)} %param.3) | copy-start | bytes 4718596
  7.2 127.3 %all-gather.2.cloned.1.call-start = ((), (), s32[]{:S(2)}) async-start(), calls=%async_computation.4 | async-start | bytes 4755456 | tf_op jit(solution)/shard_map/all_gather | solution.py:44
  9.8 138.2 %all-to-all-start.1 = ((bf16[1,128,4,384]{3,2,0,1:T(4,128)(2,1)}), bf16[1,128,4,384]{3,2,0,1:T(4,128)(2,1)S(1)}, u32[]{:S(2)}, u32[]{:S(2)}) async-start(bf16[1,128,4,384]{3,2,0,1:T(4,128)(2,1)} %reshape.42), calls=%async_computation.1 | async-start | bytes 786432 | tf_op jit(solution)/shard_map/all_to_all | solution.py:50
  147.9 43.0 %all-to-all-start = ((bf16[1,128,4,1152]{3,2,0,1:T(4,128)(2,1)}), bf16[1,128,4,1152]{3,2,0,1:T(4,128)(2,1)S(1)}, u32[]{:S(2)}, u32[]{:S(2)}) async-start(bf16[1,128,4,1152]{3,2,0,1:T(4,128)(2,1)} %bitcast.2), calls=%async_computation | async-start | bytes 2359296 | tf_op jit(solution)/shard_map/all_to_all | solution.py:49
  158.9 142.8 %reduce-scatter.2.cloned.1.call-start = ((), (), s32[]{:S(2)}) async-start(), calls=%async_computation.5 | async-start | bytes 4718592 | tf_op jit(solution)/shard_map/reduce_scatter | solution.py:73
  192.9 3.0 copy-start.1
  205.1 2.1 copy-start.3
  257.9 1.3 copy-start.2
  258.0 1341.6 %all-reduce.3.cloned.1.call-start = ((), (), s32[]{:S(2)}) async-start(), calls=%async_computation.6 | async-start | bytes 18874368
  275.0 0.7 copy-start.4
Sparse Core Ops, SparseCore 0:
  11.9 122.5 all-gather.1
  258.1 43.6 reduce-scatter.1
  304.6 1294.9 all-reduce.2
where the time goes:
time: 1620 us; the launch traced here: 1610 us
  waiting for transfers between devices  1460 us (90%)
  blocking collectives  41.1 us (3%)
  local copies, waits for them, and re-layouts  30.1 us (2%)
  matrix products  29.5 us (2%)
  starting transfers between devices  26.5 us (2%)
    unnamed x4, waiting for transfers between devices  1300 us
    all_gather x1, waiting for transfers between devices, on_device(): lax.all_gather(w_qkv, 'frames', axis=0, tiled=True).reshape(width, 3 * half)  109 us
    all_to_all x1, blocking collectives, on_device(): lax.all_to_all(patched, 'frames', split_axis=0, concat_axis=1, tiled=True)  41.1 us
  transfers between devices with their start and end apart: 5, of which 4 were waited for; matrix products, arithmetic and copies ran while one was open for 2% of the time, Pallas kernels for 0%

commit v1 on v0

v1 whole, which is shorter than its diff:
```python
import jax
import jax.numpy as jnp
from jax import lax
from jax.sharding import Mesh, PartitionSpec as P

HEAD_DIM = 64
Z, Y, XH, C, MP = 8, 4, 2, 2, 2
FR = ("z", "y", "xh", "c")
bf16, f32 = jnp.bfloat16, jnp.float32
SWAP = [(1, 2), (2, 1)]


def attend(proj, upstream):
    steps_len, count, _, half = proj.shape
    heads = half // HEAD_DIM
    scale = HEAD_DIM ** (-0.5)
    shaped = proj.reshape(steps_len, count, 3, heads, HEAD_DIM)
    query = shaped[:, :, 0]
    keys = shaped[:, :, 1]
    values = shaped[:, :, 2]
    upper = upstream.reshape(steps_len, count, heads, HEAD_DIM)
    scores = jnp.einsum("fpne,gpne->pnfg", query, keys, preferred_element_type=f32) * scale
    weights = jnp.exp(scores)
    weights = weights / jnp.sum(weights, axis=-1, keepdims=True)
    probs = weights.astype(bf16)
    dvalues = jnp.einsum("pnfg,fpne->gpne", probs, upper, preferred_element_type=f32).astype(bf16)
    dprobs = jnp.einsum("fpne,gpne->pnfg", upper, values, preferred_element_type=f32)
    center = jnp.sum(weights * dprobs, axis=-1, keepdims=True)
    dscores = (weights * (dprobs - center) * scale).astype(bf16)
    dquery = jnp.einsum("pnfg,gpne->fpne", dscores, keys, preferred_element_type=f32).astype(bf16)
    dkeys = jnp.einsum("pnfg,fpne->gpne", dscores, query, preferred_element_type=f32).astype(bf16)
    return jnp.stack([dquery, dkeys, dvalues], axis=2).reshape(steps_len, count, 3, half)


def swap_c(x):
    return lax.ppermute(x, "c", [(0, 1), (1, 0)])


def gather_weight(w):
    n = w.shape[1]
    c = lax.axis_index("c")
    xh = lax.axis_index("xh")
    other = swap_c(w)
    pair = jnp.where(c == 0, jnp.concatenate([w, other], 0), jnp.concatenate([other, w], 0))
    block = jnp.where(xh == c, pair, lax.ppermute(pair, ("xh", "c"), SWAP))
    over_z = lax.all_to_all(
        jnp.broadcast_to(block[None], (Z,) + block.shape), "z", 0, 0, tiled=True
    )
    over_y = lax.all_to_all(
        jnp.broadcast_to(over_z[None], (Y,) + over_z.shape), "y", 0, 0, tiled=True
    )
    rest = swap_c(over_y)
    mine = over_y.transpose(1, 0, 2, 3)
    rest = rest.transpose(1, 0, 2, 3)
    full = jnp.where(c == 0, jnp.stack([mine, rest], 2), jnp.stack([rest, mine], 2))
    return full.reshape(Z * Y * XH * 24, n)


def reduce_weight(term):
    n = term.shape[1]
    c = lax.axis_index("c")
    xh = lax.axis_index("xh")
    parts = term.reshape(Z, Y, XH, 24, n)
    mine = lax.dynamic_index_in_dim(parts, c, 2, keepdims=False)
    rest = lax.dynamic_index_in_dim(parts, 1 - c, 2, keepdims=False)
    total = mine.astype(f32) + swap_c(rest).astype(f32)
    total = total.astype(bf16).transpose(1, 0, 2, 3)
    got = lax.all_to_all(total, "y", 0, 0, tiled=True)
    total = jnp.sum(got.astype(f32), 0).astype(bf16)
    got = lax.all_to_all(total, "z", 0, 0, tiled=True)
    total = jnp.sum(got.astype(f32), 0)
    total = total + 0.0
    moved = lax.ppermute(total, ("xh", "c"), SWAP)
    total = jnp.where(xh == c, total, moved)
    halves = total.reshape(2, 12, n)
    mine = lax.dynamic_index_in_dim(halves, c, 0, keepdims=False)
    rest = lax.dynamic_index_in_dim(halves, 1 - c, 0, keepdims=False)
    return mine + swap_c(rest)


def on_device(normed, out_grad, w_qkv):
    frames_dev, patches, width = normed.shape
    half = out_grad.shape[2]
    out_cols = width // MP
    groups = Z * Y * XH * C
    count = patches // groups
    m = lax.axis_index("mp")
    tokens = jnp.concatenate([normed, out_grad], axis=2).reshape(groups, count, width + half)
    tokens = lax.all_to_all(tokens, FR, 0, 0, tiled=True)
    rows = tokens[:, :, :width].reshape(groups * count, width)
    upper = tokens[:, :, width:]
    weight = gather_weight(w_qkv.reshape(w_qkv.shape[0], 3 * half))

    proj = jnp.dot(rows, weight, preferred_element_type=f32).astype(bf16)
    grads = attend(proj.reshape(groups, count, 3, half), upper).reshape(groups * count, 3 * half)

    partial = lax.dot_general(
        grads, weight, (((1,), (1,)), ((), ())), preferred_element_type=f32
    ).astype(bf16)
    keep = lax.dynamic_slice_in_dim(partial, m * out_cols, out_cols, 1)
    give = lax.dynamic_slice_in_dim(partial, (1 - m) * out_cols, out_cols, 1)
    got = lax.ppermute(give, "mp", [(0, 1), (1, 0)])
    summed = (keep.astype(f32) + got.astype(f32)).astype(bf16)
    back = lax.all_to_all(summed.reshape(groups, count, out_cols), FR, 0, 0, tiled=True)
    input_grad = back.reshape(frames_dev, patches, out_cols)

    term = lax.dot_general(
        rows, grads, (((0,), (0,)), ((), ())), preferred_element_type=f32
    ).astype(bf16)
    weight_grad = reduce_weight(term) * (1.0 / groups)
    return (input_grad, weight_grad.reshape(w_qkv.shape))


def solution(mesh):
    fine = Mesh(mesh.devices.reshape(Z, Y, XH, C, MP), ("z", "y", "xh", "c", "mp"))
    in_specs = (P(FR, None, None), P(FR, None, "mp"), P(FR, None, "mp"))
    out_specs = (P(FR, None, "mp"), P(FR, None, "mp"))
    return jax.shard_map(
        on_device, mesh=fine, in_specs=in_specs, out_specs=out_specs, check_vma=False
    )
```

time: 1620 us -> 241 us (0.15)
  waiting for transfers between devices: 1460 us -> 120 us
  blocking collectives: 41.1 us -> 20.7 us
    unnamed x4 -> x0, waiting for transfers between devices: 1300 us -> none
    all_gather x1 -> x0, waiting for transfers between devices: 109 us -> none  [on_device(): lax.all_gather(w_qkv, 'frames', axis=0, tiled=True).reshape(width, 3 * half)]
    all_to_all x2 -> x5, waiting for transfers between devices: 31.6 us -> 104 us  [the longest x1 45.6 us: on_device(): tokens = lax.all_to_all(tokens, FR, 0, 0, tiled=True)]
    reduce_scatter x1 -> x0, waiting for transfers between devices: 24.8 us -> none  [on_device(): lax.psum_scatter(partial_value, 'mp', scatter_dimension=1, tiled=True)]
    all_to_all x1, blocking collectives: 41.1 us -> 20.7 us  [gather_weight(): lax.all_to_all(jnp.broadcast_to(block[None], (Z,) + block.shape), 'z', 0,...]
  transfers between devices with their start and end apart: 5 -> 12, of which waited for: 4 -> 9; matrix products, arithmetic and copies ran while one was open for 2% -> 7% of each run, Pallas kernels for 0% -> 0%
where the time goes in v1:
time: 241 us; the launch traced here: 238 us
  waiting for transfers between devices  120 us (50%)
  local copies, waits for them, and re-layouts  33.8 us (14%)
  starting transfers between devices  33 us (14%)
  blocking collectives  20.7 us (9%)
  matrix products  19.6 us (8%)
  other arithmetic  10.5 us (4%)
    all_to_all x1, waiting for transfers between devices, on_device(): tokens = lax.all_to_all(tokens, FR, 0, 0, tiled=True)  45.6 us
    all_to_all x1, blocking collectives, gather_weight(): lax.all_to_all(jnp.broadcast_to(block[None], (Z,) + block.shape), 'z', 0,...  20.7 us
    all_to_all x1, waiting for transfers between devices, reduce_weight(): got = lax.all_to_all(total, 'y', 0, 0, tiled=True)  17.4 us
    all_to_all x1, waiting for transfers between devices, on_device(): lax.all_to_all(summed.reshape(groups, count, out_cols), FR, 0, 0, tiled=T...  15.6 us
    all_to_all x1, waiting for transfers between devices, gather_weight(): lax.all_to_all(jnp.broadcast_to(over_z[None], (Y,) + over_z.shape), 'y',...  13 us
    all_to_all x1, waiting for transfers between devices, reduce_weight(): got = lax.all_to_all(total, 'z', 0, 0, tiled=True)  12.8 us
    unnamed x15, local copies, waits for them, and re-layouts  8.07 us
    all_to_all x1, starting transfers between devices, on_device(): lax.all_to_all(summed.reshape(groups, count, out_cols), FR, 0, 0, tiled=T...  7.89 us
  transfers between devices with their start and end apart: 12, of which 9 were waited for; matrix products, arithmetic and copies ran while one was open for 7% of the time, Pallas kernels for 0%

profile of v1, /device:TPU:6, one launch (start us, length us, event | category | flops | bytes accessed | tf_op | source)
XLA Modules:
  0.0 238.3 jit_solution(5861486454892217209)
XLA Ops:
  0.6 0.8 pad.13
  1.5 1.2 collective-permute-done
  2.8 3.1 %collective-permute-start.1 = (bf16[24,1152]{1,0:T(8,128)(2,1)S(1)}, bf16[24,1152]{1,0:T(8,128)(2,1)S(1)}, u32[]{:S(2)}, u32[]{:S(2)}) collective-permute-start(bf16[24,1152]{1,0:T(8,128)(2,1)S(1)} %maximum_select_fusion.1), channel_id=1, source_target_pairs={{2,4},{4,2},{3,5},{5,3},{10,12},{12,10},{11,13},{13,11},{18,20},{2... | collective-permute-start | bytes 165896 | tf_op jit(solution)/shard_map/ppermute | solution.py:45
  5.9 3.9 %collective-permute-done.1 = bf16[24,1152]{1,0:T(8,128)(2,1)S(1)} collective-permute-done((bf16[24,1152]{1,0:T(8,128)(2,1)S(1)}, bf16[24,1152]{1,0:T(8,128)(2,1)S(1)}, u32[]{:S(2)}, u32[]{:S(2)}) %collective-permute-start.1) | collective-permute-done | bytes 55328 | tf_op jit(solution)/shard_map/ppermute | solution.py:45
  9.8 20.7 %all_to_all.30 = bf16[8,24,1152]{2,1,0:T(8,128)(2,1)S(1)} all-to-all(bf16[8,24,1152]{2,1,0:T(8,128)(2,1)S(1)} %broadcast_in_dim.4), channel_id=1, replica_groups=mesh['z'=8,'y'=4,'xh'=2,'c'=2,'mp'=2] {'z'}, dimensions={0} | all-to-all | bytes 884736 | tf_op jit(solution)/shard_map/all_to_all | solution.py:46
  30.5 1.4 broadcast_in_dim.5
  31.8 4.6 %all-to-all-start.2 = ((bf16[4,8,24,1152]{3,2,1,0:T(8,128)(2,1)}), bf16[4,8,24,1152]{3,2,1,0:T(8,128)(2,1)}, u32[]{:S(2)}, u32[]{:S(2)}) async-start(bf16[4,8,24,1152]{3,2,1,0:T(8,128)(2,1)} %broadcast_in_dim.5), calls=%async_computation.2 | async-start | bytes 3538944 | tf_op jit(solution)/shard_map/all_to_all | solution.py:49
  36.4 1.1 pad_maximum_fusion
  37.6 1.5 reshape.54
  39.1 13.0 %all-to-all-done.2 = bf16[4,8,24,1152]{3,2,1,0:T(8,128)(2,1)} async-done(((bf16[4,8,24,1152]{3,2,1,0:T(8,128)(2,1)}), bf16[4,8,24,1152]{3,2,1,0:T(8,128)(2,1)}, u32[]{:S(2)}, u32[]{:S(2)}) %all-to-all-start.2) | async-done | bytes 1769504 | tf_op jit(solution)/shard_map/all_to_all | solution.py:49
  52.1 7.2 %all-to-all-start = ((bf16[128,4,1920]{2,1,0:T(4,128)(2,1)}), bf16[128,4,1920]{2,1,0:T(4,128)(2,1)S(1)}, u32[]{:S(2)}, u32[]{:S(2)}) async-start(bf16[128,4,1920]{2,1,0:T(4,128)(2,1)} %reshape.54), calls=%async_computation | async-start | bytes 3932160 | tf_op jit(solution)/shard_map/all_to_all | solution.py:89
  59.4 2.8 %copy.69 = bf16[4,8,24,1152]{3,2,0,1:T(8,128)(2,1)} copy(bf16[4,8,24,1152]{3,2,1,0:T(8,128)(2,1)} %all-to-all-done.2) | data formatting | bytes 3538944 | tf_op jit(solution)/shard_map/all_to_all | solution.py:49
  62.4 45.6 %all-to-all-done = bf16[128,4,1920]{2,1,0:T(4,128)(2,1)S(1)} async-done(((bf16[128,4,1920]{2,1,0:T(4,128)(2,1)}), bf16[128,4,1920]{2,1,0:T(4,128)(2,1)S(1)}, u32[]{:S(2)}, u32[]{:S(2)}) %all-to-all-start) | async-done | bytes 1966112 | tf_op jit(solution)/shard_map/all_to_all | solution.py:89
  108.1 1.0 copy.46
  110.0 3.9 %maximum_select_fusion = bf16[8,4,2,24,1152]{4,3,2,1,0:T(8,128)(2,1)S(1)} fusion(bf16[8,4,1,24,1152]{4,3,2,1,0:T(8,128)(2,1)} %bitcast.3, bf16[8,4,1,24,1152]{4,3,2,1,0:T(8,128)(2,1)} %bitcast.66, pred[]{:T(512)S(6)} %eq.8), kind=kLoop, calls=%fused_computation.2 | loop fusion | flops 5308416 | bytes 7077889 | tf_op jit(solution)/shard_map/jit(_where)/select_n | solution.py:55
  114.0 1.8 copy-done.1
  115.7 3.3 %convolution_convert_fusion.2 = bf16[512,1152]{1,0:T(8,128)(2,1)} fusion(bf16[512,1536]{1,0:T(8,128)(2,1)S(1)} %reshape.55, bf16[1536,1152]{1,0:T(8,128)(2,1)S(1)} %bitcast.67), kind=kOutput, calls=%fused_computation.6 | convolution fusion | flops 1812529152 | bytes 6291456 | tf_op jit(solution)/shard_map/dot_general | solution.py:94
  119.0 3.3 %reshape_reshape.6 = bf16[128,4,3,6,64]{4,3,2,1,0:T(8,128)(2,1)S(1)} reshape(bf16[512,1152]{1,0:T(8,128)(2,1)} %convolution_convert_fusion.2) | data formatting | bytes 2359296 | tf_op jit(solution)/shard_map/reshape;reshape | solution.py:17
  122.3 1.9 fusion.41
  124.2 2.1 copy.58
  126.3 2.0 copy.57
  128.4 0.9 copy.59
  129.3 0.6 fusion.27
  130.3 0.6 fusion.24
  130.9 1.6 fusion.30
  132.6 2.5 %fusion.18 = bf16[128,4,1,6,64]{0,4,3,1,2:T(8,128)(2,1)S(1)} fusion(f32[4,6,128,128]{2,3,1,0:T(8,128)S(1)} %fusion.27, f32[4,6,128,128]{2,3,1,0:T(8,128)} %fusion.30, bf16[128,4,1,6,64]{0,4,3,1,2:T(8,128)(2,1)S(1)} %copy.58), kind=kOutput, calls=%fused_computation.21 | convolution fusion | flops 52497536 | bytes 3932160 | tf_op jit(solution)/shard_map/pnfg,fpne->gpne/dot_general | solution.py:31
  135.1 2.4 %fusion.21 = bf16[128,4,1,6,64]{0,4,3,1,2:T(8,128)(2,1)S(1)} fusion(f32[4,6,128,128]{2,3,1,0:T(8,128)S(1)} %fusion.27, f32[4,6,128,128]{2,3,1,0:T(8,128)} %fusion.30, bf16[128,4,1,6,64]{0,4,3,1,2:T(8,128)(2,1)S(1)} %copy.57), kind=kOutput, calls=%fused_computation.22 | convolution fusion | flops 52497536 | bytes 3932160 | tf_op jit(solution)/shard_map/pnfg,gpne->fpne/dot_general | solution.py:30
  137.5 1.2 pad_maximum_fusion.1
  138.7 5.5 %copy.51 = bf16[128,4,3,6,64]{4,3,2,1,0:T(8,128)(2,1)S(1)} copy(bf16[128,4,3,6,64]{0,4,3,1,2:T(8,128)(2,1)} %pad_maximum_fusion.1) | data formatting | bytes 2359296 | tf_op jit(solution)/shard_map/stack | solution.py:32
  144.2 2.9 %reshape_reshape.7 = bf16[512,1152]{1,0:T(8,128)(2,1)} reshape(bf16[128,4,3,6,64]{4,3,2,1,0:T(8,128)(2,1)S(1)} %copy.51) | data formatting | bytes 2359296 | tf_op jit(solution)/shard_map/reshape;reshape | solution.py:95
  147.2 4.0 %convolution_convert_fusion = bf16[1536,1152]{1,0:T(8,128)(2,1)S(1)} fusion(bf16[512,1536]{1,0:T(8,128)(2,1)} %copy-done.3, bf16[512,1152]{1,0:T(8,128)(2,1)} %reshape_reshape.7), kind=kOutput, calls=%fused_computation.1 | convolution fusion | flops 1813708800 | bytes 6291456 | tf_op jit(solution)/shard_map/dot_general | solution.py:107
  151.8 3.7 %collective-permute-done.4 = bf16[8,4,24,1152]{3,2,0,1:T(8,128)(2,1)S(1)} collective-permute-done((bf16[8,4,24,1152]{3,2,0,1:T(8,128)(2,1)S(1)}, bf16[8,4,24,1152]{3,2,0,1:T(8,128)(2,1)S(1)}, u32[]{:S(2)}, u32[]{:S(2)}) %collective-permute-start.4) | collective-permute-done | bytes 1769504 | tf_op jit(solution)/shard_map/ppermute | solution.py:36
  155.5 1.7 fusion.2
  157.2 3.6 %all-to-all-start.4 = ((bf16[4,8,24,1152]{3,2,1,0:T(8,128)(2,1)}), bf16[4,8,24,1152]{3,2,1,0:T(8,128)(2,1)S(1)}, u32[]{:S(2)}, u32[]{:S(2)}) async-start(bf16[4,8,24,1152]{3,2,1,0:T(8,128)(2,1)} %fusion.2), calls=%async_computation.4 | async-start | bytes 3538944 | tf_op jit(solution)/shard_map/all_to_all | solution.py:68
  160.8 4.6 %convolution_convert_fusion.1 = bf16[512,1536]{1,0:T(8,128)(2,1)S(1)} fusion(bf16[512,1152]{1,0:T(8,128)(2,1)} %reshape_reshape.7, bf16[1536,1152]{1,0:T(8,128)(2,1)} %bitcast.68), kind=kOutput, calls=%fused_computation.5 | convolution fusion | flops 1812725760 | bytes 6291456 | tf_op jit(solution)/shard_map/dot_general | solution.py:97
  165.4 0.9 constant_dynamic-slice_fusion.2
  166.8 17.4 %all-to-all-done.4 = bf16[4,8,24,1152]{3,2,1,0:T(8,128)(2,1)S(1)} async-done(((bf16[4,8,24,1152]{3,2,1,0:T(8,128)(2,1)}), bf16[4,8,24,1152]{3,2,1,0:T(8,128)(2,1)S(1)}, u32[]{:S(2)}, u32[]{:S(2)}) %all-to-all-start.4) | async-done | bytes 1769504 | tf_op jit(solution)/shard_map/all_to_all | solution.py:68
  184.1 1.1 reduce_sum.41
  185.3 3.8 %all-to-all-start.5 = ((bf16[8,24,1152]{2,1,0:T(8,128)(2,1)}), bf16[8,24,1152]{2,1,0:T(8,128)(2,1)S(1)}, u32[]{:S(2)}, u32[]{:S(2)}) async-start(bf16[8,24,1152]{2,1,0:T(8,128)(2,1)} %reduce_sum.41), calls=%async_computation.5 | async-start | bytes 884736 | tf_op jit(solution)/shard_map/all_to_all | solution.py:70
  189.0 1.3 add_convert_fusion
  190.4 1.1 reshape.58
  191.4 12.8 %all-to-all-done.5 = bf16[8,24,1152]{2,1,0:T(8,128)(2,1)S(1)} async-done(((bf16[8,24,1152]{2,1,0:T(8,128)(2,1)}), bf16[8,24,1152]{2,1,0:T(8,128)(2,1)S(1)}, u32[]{:S(2)}, u32[]{:S(2)}) %all-to-all-start.5) | async-done | bytes 442400 | tf_op jit(solution)/shard_map/all_to_all | solution.py:70
  204.2 7.9 %all-to-all-start.3 = ((bf16[128,4,768]{2,1,0:T(4,128)(2,1)}), bf16[128,4,768]{2,1,0:T(4,128)(2,1)S(1)}, u32[]{:S(2)}, u32[]{:S(2)}) async-start(bf16[128,4,768]{2,1,0:T(4,128)(2,1)} %reshape.58), calls=%async_computation.3 | async-start | bytes 1572864 | tf_op jit(solution)/shard_map/all_to_all | solution.py:104
  212.2 2.0 collective-permute-start.5
  214.2 6.5 %collective-permute-done.5 = f32[24,1152]{1,0:T(8,128)S(1)} collective-permute-done((f32[24,1152]{1,0:T(8,128)S(1)}, f32[24,1152]{1,0:T(8,128)S(1)}, u32[]{:S(2)}, u32[]{:S(2)}) %collective-permute-start.5) | collective-permute-done | bytes 110624 | tf_op jit(solution)/shard_map/ppermute | solution.py:73
  220.9 15.6 %all-to-all-done.3 = bf16[128,4,768]{2,1,0:T(4,128)(2,1)S(1)} async-done(((bf16[128,4,768]{2,1,0:T(4,128)(2,1)}), bf16[128,4,768]{2,1,0:T(4,128)(2,1)S(1)}, u32[]{:S(2)}, u32[]{:S(2)}) %all-to-all-start.3) | async-done | bytes 786464 | tf_op jit(solution)/shard_map/all_to_all | solution.py:104
  236.5 1.1 reshape.59
  237.6 0.7 reshape.62
  (31 shorter events, 3.1 us)
Async XLA Ops:
  1.4 1.3 collective-permute-start
  2.8 7.0 %collective-permute-start.1 = (bf16[24,1152]{1,0:T(8,128)(2,1)S(1)}, bf16[24,1152]{1,0:T(8,128)(2,1)S(1)}, u32[]{:S(2)}, u32[]{:S(2)}) collective-permute-start(bf16[24,1152]{1,0:T(8,128)(2,1)S(1)} %maximum_select_fusion.1), channel_id=1, source_target_pairs={{2,4},{4,2},{3,5},{5,3},{10,12},{12,10},{11,13},{13,11},{18,20},{2... | collective-permute-start | bytes 165896 | tf_op jit(solution)/shard_map/ppermute | solution.py:45
  31.8 4.6 %copy-start.4 = (bf16[1,512,1536]{2,1,0:T(8,128)(2,1)S(1)}, bf16[1,512,1536]{2,1,0:T(8,128)(2,1)}, u32[]{:S(2)}) copy-start(bf16[1,512,1536]{2,1,0:T(8,128)(2,1)} %param.3) | copy-start | bytes 4718596
  31.8 20.3 %all-to-all-start.2 = ((bf16[4,8,24,1152]{3,2,1,0:T(8,128)(2,1)}), bf16[4,8,24,1152]{3,2,1,0:T(8,128)(2,1)}, u32[]{:S(2)}, u32[]{:S(2)}) async-start(bf16[4,8,24,1152]{3,2,1,0:T(8,128)(2,1)} %broadcast_in_dim.5), calls=%async_computation.2 | async-start | bytes 3538944 | tf_op jit(solution)/shard_map/all_to_all | solution.py:49
  52.1 55.8 %all-to-all-start = ((bf16[128,4,1920]{2,1,0:T(4,128)(2,1)}), bf16[128,4,1920]{2,1,0:T(4,128)(2,1)S(1)}, u32[]{:S(2)}, u32[]{:S(2)}) async-start(bf16[128,4,1920]{2,1,0:T(4,128)(2,1)} %reshape.54), calls=%async_computation | async-start | bytes 3932160 | tf_op jit(solution)/shard_map/all_to_all | solution.py:89
  62.2 47.8 %collective-permute-start.2 = (bf16[4,8,24,1152]{3,2,0,1:T(8,128)(2,1)}, bf16[4,8,24,1152]{3,2,0,1:T(8,128)(2,1)}, u32[]{:S(2)}, u32[]{:S(2)}) collective-permute-start(bf16[4,8,24,1152]{3,2,0,1:T(8,128)(2,1)} %copy.69), channel_id=1, source_target_pairs={{0,2},{2,0},{1,3},{3,1},{4,6},{6,4},{5,7},{7,5},{8,10},{10,8},{9,1... | collective-permute-start | bytes 5308424 | tf_op jit(solution)/shard_map/ppermute | solution.py:36
  110.0 4.0 %copy-start.3 = (bf16[512,1536]{1,0:T(8,128)(2,1)}, bf16[512,1536]{1,0:T(8,128)(2,1)S(1)}, u32[]{:S(2)}) copy-start(bf16[512,1536]{1,0:T(8,128)(2,1)S(1)} %reshape.55) | copy-start | bytes 4718596
  113.9 1.8 copy-start.1
  124.2 4.2 %copy-start = (bf16[128,4,1,6,64]{4,3,2,1,0:T(8,128)(2,1)S(1)}, bf16[128,4,1,6,64]{4,3,2,1,0:T(8,128)(2,1)}, u32[]{:S(2)}) copy-start(bf16[128,4,1,6,64]{4,3,2,1,0:T(8,128)(2,1)} %get-tuple-element.4) | copy-start | bytes 1179652
  129.3 1.0 copy-start.2
  151.7 3.8 %collective-permute-start.4 = (bf16[8,4,24,1152]{3,2,0,1:T(8,128)(2,1)S(1)}, bf16[8,4,24,1152]{3,2,0,1:T(8,128)(2,1)S(1)}, u32[]{:S(2)}, u32[]{:S(2)}) collective-permute-start(bf16[8,4,24,1152]{3,2,0,1:T(8,128)(2,1)S(1)} %bitcast.72), channel_id=1, source_target_pairs={{0,2},{2,0},{1,3},{3,1},{4,6},{6,4},{5,7},{7,5},{8,10},{10,8},{9,1... | collective-permute-start | bytes 5308424 | tf_op jit(solution)/shard_map/ppermute | solution.py:36
  157.2 27.0 %all-to-all-start.4 = ((bf16[4,8,24,1152]{3,2,1,0:T(8,128)(2,1)}), bf16[4,8,24,1152]{3,2,1,0:T(8,128)(2,1)S(1)}, u32[]{:S(2)}, u32[]{:S(2)}) async-start(bf16[4,8,24,1152]{3,2,1,0:T(8,128)(2,1)} %fusion.2), calls=%async_computation.4 | async-start | bytes 3538944 | tf_op jit(solution)/shard_map/all_to_all | solution.py:68
  166.3 22.7 %collective-permute-start.3 = (bf16[512,768]{1,0:T(8,128)(2,1)}, bf16[512,768]{1,0:T(8,128)(2,1)}, u32[]{:S(2)}, u32[]{:S(2)}) collective-permute-start(bf16[512,768]{1,0:T(8,128)(2,1)} %constant_dynamic-slice_fusion.2), channel_id=1, source_target_pairs={{0,1},{1,0},{2,3},{3,2},{4,5},{5,4},{6,7},{7,6},{8,9},{9,8},{10,11... | collective-permute-start | bytes 2359304 | tf_op jit(solution)/shard_map/ppermute | solution.py:102
  185.3 19.0 %all-to-all-start.5 = ((bf16[8,24,1152]{2,1,0:T(8,128)(2,1)}), bf16[8,24,1152]{2,1,0:T(8,128)(2,1)S(1)}, u32[]{:S(2)}, u32[]{:S(2)}) async-start(bf16[8,24,1152]{2,1,0:T(8,128)(2,1)} %reduce_sum.41), calls=%async_computation.5 | async-start | bytes 884736 | tf_op jit(solution)/shard_map/all_to_all | solution.py:70
  204.2 32.3 %all-to-all-start.3 = ((bf16[128,4,768]{2,1,0:T(4,128)(2,1)}), bf16[128,4,768]{2,1,0:T(4,128)(2,1)S(1)}, u32[]{:S(2)}, u32[]{:S(2)}) async-start(bf16[128,4,768]{2,1,0:T(4,128)(2,1)} %reshape.58), calls=%async_computation.3 | async-start | bytes 1572864 | tf_op jit(solution)/shard_map/all_to_all | solution.py:104
  212.2 8.5 %collective-permute-start.5 = (f32[24,1152]{1,0:T(8,128)S(1)}, f32[24,1152]{1,0:T(8,128)S(1)}, u32[]{:S(2)}, u32[]{:S(2)}) collective-permute-start(f32[24,1152]{1,0:T(8,128)S(1)} %convert_reduce_fusion), channel_id=1, source_target_pairs={{2,4},{4,2},{3,5},{5,3},{10,12},{12,10},{11,13},{13,11},{18,20},{2... | collective-permute-start | bytes 331784 | tf_op jit(solution)/shard_map/ppermute | solution.py:73
  220.8 16.8 %collective-permute-start.6 = (f32[12,1152]{1,0:T(8,128)S(1)}, f32[12,1152]{1,0:T(8,128)S(1)}, u32[]{:S(2)}, u32[]{:S(2)}) collective-permute-start(f32[12,1152]{1,0:T(8,128)S(1)} %dynamic-slice_bitcast_fusion), channel_id=1, source_target_pairs={{0,2},{2,0},{1,3},{3,1},{4,6},{6,4},{5,7},{7,5},{8,10},{10,8},{9,1... | collective-permute-start | bytes 165896 | tf_op jit(solution)/shard_map/ppermute | solution.py:36
